TPU v7x, 32 devices: a whole 2x2x4 slice. The times are simulated.
32 devices in a mesh: dp: 4 (over z), row: 2 (over core), col: 4 (over y, x).
Axes of the slice: x: 2, y: 2, z: 4, core: 2. Of those that a mesh axis runs over, the one named last changes fastest.
Arguments:
- features: bfloat16 [2048, 4096], P(('dp', 'row')), may hold values from -6 to 6
- w_in: bfloat16 [4096, 4096], P('row', 'col'), may hold values from -0.09375 to 0.09375
- w_out: bfloat16 [4096, 1024], P('col'), may hold values from -0.09375 to 0.09375
- captions: bfloat16 [2048, 1024], P(('dp', 'row', 'col')), may hold values from -6 to 6
- positive: int32 [2048], P(('dp', 'row')), may hold values from 0 to 2047, each once
Outputs:
- fig_terms: float32 [2048], P(('dp', 'row'))
- cap_terms: float32 [2048], P(('dp', 'row', 'col'))
- grad_w_in: float32 [4096, 4096], P(('dp', 'row'), 'col')
- grad_w_out: float32 [4096, 1024], P('col', ('dp', 'row'))
Inputs may be any that keep to these rules, and one draw needn't show every extreme that they name: positive is a permutation: every caption is the match of exactly one figure.
All inputs are finite; a program needn't handle non-finite values.
Results may differ from a plain program's by a relative error of at most 0.0053.
Values may be sent and summed in bfloat16 or wider, within the bound.
A program may use at most 128 MiB of HBM per device.

v0:
```python
import jax
import jax.numpy as jnp
from jax import lax
from jax.sharding import PartitionSpec as P

SCALE = 50.0
EPS = 1e-06


def gelu_back(pre, grad):
    return jax.vjp(jax.nn.gelu, pre)[1](grad)[0]


def on_device(features, w_in, w_out, captions, positive):
    columns = features
    pre = jnp.dot(
        columns, lax.all_gather(w_in, "row", axis=0, tiled=True), preferred_element_type=jnp.float32
    )
    hidden = jax.nn.gelu(pre).astype(jnp.bfloat16)
    emb = lax.psum(jnp.dot(hidden, w_out, preferred_element_type=jnp.float32), "col")
    inv = lax.rsqrt(jnp.sum(emb * emb, axis=1, keepdims=True) + EPS)
    fhat = emb * inv
    fhat_b = fhat.astype(jnp.bfloat16)
    cap32 = captions.astype(jnp.float32)
    chat_local = (cap32 * lax.rsqrt(jnp.sum(cap32 * cap32, axis=1, keepdims=True) + EPS)).astype(
        jnp.bfloat16
    )
    block = lax.all_gather(chat_local, ("dp", "row"), axis=0, tiled=True)
    capdev = captions.shape[0]
    ncol = lax.axis_size("col")
    places = jnp.arange(block.shape[0], dtype=jnp.int32)
    colids = (places // capdev * ncol + lax.axis_index("col")) * capdev + places % capdev
    logits = SCALE * lax.dot_general(
        fhat_b, block, (((1,), (1,)), ((), ())), preferred_element_type=jnp.float32
    )
    mask = (positive[:, None] == colids[None, :]).astype(jnp.float32)
    expo = jnp.exp(logits)
    picked = mask * logits
    rowsum, rowpos = lax.psum((jnp.sum(expo, axis=1), jnp.sum(picked, axis=1)), "col")
    colsum, colpos = lax.psum((jnp.sum(expo, axis=0), jnp.sum(picked, axis=0)), ("dp", "row"))
    fig_terms = jnp.log(rowsum) - rowpos
    group = lax.axis_index("dp") * lax.axis_size("row") + lax.axis_index("row")
    cap_all = jnp.log(colsum) - colpos
    cap_terms = lax.dynamic_slice_in_dim(cap_all, group * capdev, capdev, 0)
    dlog = (expo / rowsum[:, None] + expo / colsum[None, :] - 2.0 * mask).astype(jnp.bfloat16)
    direction = SCALE * jnp.dot(dlog, block, preferred_element_type=jnp.float32)
    dfhat = lax.psum(direction, "col")
    demb = ((dfhat - fhat * jnp.sum(fhat * dfhat, axis=1, keepdims=True)) * inv).astype(
        jnp.bfloat16
    )
    dh = lax.dot_general(demb, w_out, (((1,), (1,)), ((), ())), preferred_element_type=jnp.float32)
    dpre = gelu_back(pre, dh).astype(jnp.bfloat16)
    head_term = lax.dot_general(
        hidden, demb, (((0,), (0,)), ((), ())), preferred_element_type=jnp.float32
    )
    grad_w_out = lax.psum_scatter(head_term, ("dp", "row"), scatter_dimension=1, tiled=True)
    columns = features
    grad_w_in = lax.psum_scatter(
        lax.dot_general(
            columns, dpre, (((0,), (0,)), ((), ())), preferred_element_type=jnp.float32
        ),
        ("dp", "row"),
        scatter_dimension=0,
        tiled=True,
    )
    return (fig_terms, cap_terms, grad_w_in, grad_w_out)


def solution(mesh):
    placed = (
        P(("dp", "row"), None),
        P("row", "col"),
        P("col", None),
        P(("dp", "row", "col"), None),
        P(("dp", "row")),
    )
    return jax.shard_map(
        on_device,
        mesh=mesh,
        in_specs=placed,
        out_specs=(
            P(("dp", "row")),
            P(("dp", "row", "col")),
            P(("dp", "row"), "col"),
            P("col", ("dp", "row")),
        ),
        check_vma=False,
    )
```

profile of v0, /device:TPU:0, one launch (start us, length us, event | category | flops | bytes accessed | tf_op | source)
XLA Modules:
  0.0 419.0 jit_solution(432756732322447782)
XLA Ops:
  8.1 0.7 all-gather.3.cloned.1.call-update
  8.8 24.2 %all-gather.3.cloned.1.call-done = bf16[4096,1024]{1,0:T(8,128)(2,1)} async-done(((bf16[2048,1024]{1,0:T(8,128)(2,1)}), bf16[4096,1024]{1,0:T(8,128)(2,1)}) %all-gather.3.cloned.1.call-update) | async-done | bytes 8388624 | tf_op jit(solution)/shard_map/all_gather | solution.py:17
  33.0 6.3 %fusion.51 = f32[256,1024]{1,0:T(8,128)S(1)} fusion(bf16[256,4096]{1,0:T(8,128)(2,1)} %param.5, bf16[4096,1024]{1,0:T(8,128)(2,1)} %all-gather.3.cloned.1.call-done), kind=kOutput, calls=%fused_computation.72 | convolution fusion | flops 2147483648 | bytes 11534336 | tf_op jit(solution)/shard_map/dot_general | solution.py:16
  39.3 1.0 copy-done.4
  40.3 1.8 fusion.48
  42.2 0.1 fusion.20
  42.4 0.8 fusion.21
  43.2 52.8 %all-reduce.5.cloned.1.call-done = f32[256,1024]{1,0:T(8,128)} async-done(((f32[256,1024]{1,0:T(8,128)}), f32[256,1024]{1,0:T(8,128)}) %all-reduce.5.cloned.1.call-update) | async-done | bytes 1048592 | tf_op jit(solution)/shard_map/psum | solution.py:20
  96.0 1.4 multiply_reduce_fusion.1
  97.5 2.9 fusion.17
  100.4 16.3 %all-reduce = (f32[512]{0:T(512)S(1)}, f32[512]{0:T(512)S(1)}) all-reduce(f32[512]{0:T(512)S(1)} %get-tuple-element.8, f32[512]{0:T(512)S(1)} %get-tuple-element.10), channel_id=1, replica_groups=mesh['dp'=4,'row'=2,'col'=4] {'dp','row'}, use_global_device_ids=true, to_apply=%region_10.11 | all-reduce | flops 1024 | bytes 8192 | tf_op jit(solution)/shard_map/psum | solution.py:40
  116.7 8.9 %all-reduce.1 = (f32[256]{0:T(256)S(1)}, f32[256]{0:T(256)S(1)}) all-reduce(f32[256]{0:T(256)S(1)} %get-tuple-element.9, f32[256]{0:T(256)S(1)} %get-tuple-element.11), channel_id=1, replica_groups=mesh['dp'=4,'row'=2,'col'=4] {'col'}, use_global_device_ids=true, to_apply=%region_6.7 | all-reduce | flops 512 | bytes 4096 | tf_op jit(solution)/shard_map/psum | solution.py:39
  125.6 3.0 convolution_multiply_fusion
  128.7 49.9 %all-reduce.7.cloned.1.call-done = f32[256,1024]{1,0:T(8,128)} async-done(((f32[256,1024]{1,0:T(8,128)}), f32[256,1024]{1,0:T(8,128)}) %all-reduce.7.cloned.1.call-update) | async-done | bytes 1048592 | tf_op jit(solution)/shard_map/psum | solution.py:47
  178.6 1.6 multiply_reduce_fusion
  180.2 1.0 multiply_convert_fusion
  181.2 11.2 %convolution_bitcast_fusion = f32[4096,1024]{0,1:T(8,128)} fusion(bf16[256,4096]{1,0:T(8,128)(2,1)} %param.5, f32[256,1024]{1,0:T(8,128)} %copy-done.4, bf16[256,1024]{1,0:T(8,128)(2,1)} %multiply_convert_fusion, bf16[1024,1024]{1,0:T(8,128)(2,1)S(1)} %copy-done), kind=kOutput, calls=%fused_computation | convolution fusion | flops 2689597440 | bytes 22544384 | tf_op jit(solution)/shard_map/dot_general | solution.py:59
  192.5 1.0 copy-done.2
  193.5 4.0 fusion.47
  197.5 0.6 dynamic_slice.3
  198.1 0.6 log_subtract_fusion.1
  198.7 161.9 %reduce-scatter.3.cloned.1.call-done = f32[512,1024]{0,1:T(8,128)} async-done(((f32[4096,1024]{0,1:T(8,128)}), f32[512,1024]{0,1:T(8,128)}) %reduce-scatter.3.cloned.1.call-update) | async-done | bytes 2097168 | tf_op jit(solution)/shard_map/reduce_scatter | solution.py:58
  360.6 2.9 copy.9
  363.5 48.1 %reduce-scatter.5.cloned.1.call-done = f32[1024,128]{1,0:T(8,128)} async-done(((f32[1024,1024]{1,0:T(8,128)}), f32[1024,128]{1,0:T(8,128)}) %reduce-scatter.5.cloned.1.call-update) | async-done | bytes 524304 | tf_op jit(solution)/shard_map/reduce_scatter | solution.py:56
  (28 shorter events, 0.4 us)
Async XLA Ops:
  8.0 32.3 %copy-start = (bf16[1024,1024]{1,0:T(8,128)(2,1)S(1)}, bf16[1024,1024]{1,0:T(8,128)(2,1)}, u32[]{:S(2)}) copy-start(bf16[1024,1024]{1,0:T(8,128)(2,1)} %param.7) | copy-start | bytes 6291460
  8.0 25.0 %all-gather.3.cloned.1.call-start = ((), (), s32[]{:S(2)}) async-start(), calls=%async_computation.2 | async-start | bytes 12582912 | tf_op jit(solution)/shard_map/all_gather | solution.py:17
  8.7 87.3 %all-reduce.5.cloned.1.call-start = ((), (), s32[]{:S(2)}) async-start(), calls=%async_computation.3 | async-start | bytes 2097152 | tf_op jit(solution)/shard_map/psum | solution.py:20
  39.3 1.0 copy-start.4
  40.3 1.9 copy-start.5
  42.1 55.3 %copy-start.6 = (s32[256]{0:T(256)S(1)}, s32[256]{0:T(256)}, u32[]{:S(2)}) copy-start(s32[256]{0:T(256)} %param.9) | copy-start | bytes 3076
  42.2 55.3 %all-gather.5.cloned.1.call-start = ((), (), s32[]{:S(2)}) async-start(), calls=%async_computation.4 | async-start | bytes 1179648 | tf_op jit(solution)/shard_map/all_gather | solution.py:28
  43.1 135.4 %all-reduce.7.cloned.1.call-start = ((), (), s32[]{:S(2)}) async-start(), calls=%async_computation.5 | async-start | bytes 2097152 | tf_op jit(solution)/shard_map/psum | solution.py:47
  125.6 53.0 %copy-start.1 = (f32[256,1024]{1,0:T(8,128)S(1)}, f32[256,1024]{1,0:T(8,128)}, u32[]{:S(2)}) copy-start(f32[256,1024]{1,0:T(8,128)} %all-reduce.5.cloned.1.call-done) | copy-start | bytes 3145732
  128.6 232.0 %reduce-scatter.3.cloned.1.call-start = ((), (), s32[]{:S(2)}) async-start(), calls=%async_computation.6 | async-start | bytes 18874368 | tf_op jit(solution)/shard_map/reduce_scatter | solution.py:58
  178.6 1.6 copy-start.3
  192.4 1.0 copy-start.2
  192.4 219.2 %reduce-scatter.5.cloned.1.call-start = ((), (), s32[]{:S(2)}) async-start(), calls=%async_computation.7 | async-start | bytes 4718592 | tf_op jit(solution)/shard_map/reduce_scatter | solution.py:56
Sparse Core Ops, SparseCore 0:
  10.4 22.5 all-gather.2
  42.3 53.7 all-reduce.4
  128.8 49.7 all-reduce.6
Sparse Core Ops, SparseCore 1:
  44.8 23.1 all-gather.4
  192.5 168.0 reduce-scatter.2
  363.3 48.2 reduce-scatter.4
where the time goes:
time: 419 us
  waiting for transfers between devices  338 us (81%)
  matrix products  29.3 us (7%)
  blocking collectives  25.2 us (6%)
  between operations  15.5 us (4%)
  local copies, waits for them, and re-layouts  5.45 us (1%)
  other arithmetic  5.45 us (1%)
    reduce_scatter x1, waiting for transfers between devices, on_device(): lax.psum_scatter(lax.dot_general(columns, dpre, (((0,), (0,)), ((), ())),...  162 us
    psum x1, waiting for transfers between devices, on_device(): lax.psum(jnp.dot(hidden, w_out, preferred_element_type=jnp.float32), 'col')  52.8 us
    psum x1, waiting for transfers between devices, on_device(): dfhat = lax.psum(direction, 'col')  49.9 us
    reduce_scatter x1, waiting for transfers between devices, on_device(): lax.psum_scatter(head_term, ('dp', 'row'), scatter_dimension=1, tiled=True)  48.1 us
    all_gather x1, waiting for transfers between devices, on_device(): lax.all_gather(w_in, 'row', axis=0, tiled=True)  24.2 us
    psum x1, blocking collectives, on_device(): lax.psum((jnp.sum(expo, axis=0), jnp.sum(picked, axis=0)), ('dp', 'row'))  16.3 us
    dot_general x1, matrix products, on_device(): lax.dot_general(columns, dpre, (((0,), (0,)), ((), ())), preferred_elemen...  11.2 us
    psum x1, blocking collectives, on_device(): lax.psum((jnp.sum(expo, axis=1), jnp.sum(picked, axis=1)), 'col')  8.92 us
  transfers between devices with their start and end apart: 6, of which 5 were waited for; matrix products, arithmetic and copies ran while one was open for 2% of the time, Pallas kernels for 0%

commit v1 on v0

--- a/solution.py
+++ b/solution.py
@@ -17,7 +17,9 @@
         columns, lax.all_gather(w_in, "row", axis=0, tiled=True), preferred_element_type=jnp.float32
     )
     hidden = jax.nn.gelu(pre).astype(jnp.bfloat16)
-    emb = lax.psum(jnp.dot(hidden, w_out, preferred_element_type=jnp.float32), "col")
+    emb = jnp.sum(
+        lax.all_gather(jnp.dot(hidden, w_out, preferred_element_type=jnp.float32), "col"), axis=0
+    )
     inv = lax.rsqrt(jnp.sum(emb * emb, axis=1, keepdims=True) + EPS)
     fhat = emb * inv
     fhat_b = fhat.astype(jnp.bfloat16)

time: 419 us -> 440 us (1.050)
  waiting for transfers between devices: 338 us -> 359 us
    all_gather x0 -> x1, waiting for transfers between devices: none -> 53 us  [on_device(): lax.all_gather(jnp.dot(hidden, w_out, preferred_element_type=jnp.float32)...]
    psum x1 -> x0, waiting for transfers between devices: 52.8 us -> none  [on_device(): lax.psum(jnp.dot(hidden, w_out, preferred_element_type=jnp.float32), 'col')]
    all_gather x1, waiting for transfers between devices: 0.02 us -> 21.4 us  [on_device(): block = lax.all_gather(chat_local, ('dp', 'row'), axis=0, tiled=True)]
  transfers between devices with their start and end apart: 6 -> 6, of which waited for: 5 -> 6; matrix products, arithmetic and copies ran while one was open for 2% -> 3% of each run, Pallas kernels for 0% -> 0%
where the time goes in v1:
time: 440 us
  waiting for transfers between devices  359 us (82%)
  matrix products  28.9 us (7%)
  blocking collectives  25.1 us (6%)
  between operations  14.2 us (3%)
  other arithmetic  6.94 us (2%)
  local copies, waits for them, and re-layouts  5.45 us (1%)
    reduce_scatter x1, waiting for transfers between devices, on_device(): lax.psum_scatter(lax.dot_general(columns, dpre, (((0,), (0,)), ((), ())),...  162 us
    all_gather x1, waiting for transfers between devices, on_device(): lax.all_gather(jnp.dot(hidden, w_out, preferred_element_type=jnp.float32)...  53 us
    psum x1, waiting for transfers between devices, on_device(): dfhat = lax.psum(direction, 'col')  49 us
    reduce_scatter x1, waiting for transfers between devices, on_device(): lax.psum_scatter(head_term, ('dp', 'row'), scatter_dimension=1, tiled=True)  48.2 us
    all_gather x1, waiting for transfers between devices, on_device(): lax.all_gather(w_in, 'row', axis=0, tiled=True)  24.2 us
    all_gather x1, waiting for transfers between devices, on_device(): block = lax.all_gather(chat_local, ('dp', 'row'), axis=0, tiled=True)  21.4 us
    psum x1, blocking collectives, on_device(): lax.psum((jnp.sum(expo, axis=0), jnp.sum(picked, axis=0)), ('dp', 'row'))  15.4 us
    dot_general x1, matrix products, on_device(): lax.dot_general(columns, dpre, (((0,), (0,)), ((), ())), preferred_elemen...  11.2 us
  transfers between devices with their start and end apart: 6, of which 6 were waited for; matrix products, arithmetic and copies ran while one was open for 3% of the time, Pallas kernels for 0%

profile of v1, /device:TPU:0, one launch (start us, length us, event | category | flops | bytes accessed | tf_op | source)
XLA Modules:
  0.0 439.5 jit_solution(6842506910020399564)
XLA Ops:
  7.2 0.7 all-gather.5.cloned.1.call-update
  8.0 24.2 %all-gather.5.cloned.1.call-done = bf16[4096,1024]{1,0:T(8,128)(2,1)} async-done(((bf16[2048,1024]{1,0:T(8,128)(2,1)}), bf16[4096,1024]{1,0:T(8,128)(2,1)}) %all-gather.5.cloned.1.call-update) | async-done | bytes 8388624 | tf_op jit(solution)/shard_map/all_gather | solution.py:17
  32.1 6.3 %fusion.51 = f32[256,1024]{1,0:T(8,128)S(1)} fusion(bf16[256,4096]{1,0:T(8,128)(2,1)} %param.5, bf16[4096,1024]{1,0:T(8,128)(2,1)} %all-gather.5.cloned.1.call-done), kind=kOutput, calls=%fused_computation.72 | convolution fusion | flops 2147483648 | bytes 11534336 | tf_op jit(solution)/shard_map/dot_general | solution.py:16
  38.5 1.0 copy-done.3
  39.5 1.8 fusion.48
  41.5 0.8 fusion.21
  42.4 53.0 %all-gather.9.cloned.1.call-done = f32[1024,1024]{1,0:T(8,128)} async-done(((f32[256,1024]{1,0:T(8,128)}), f32[1024,1024]{1,0:T(8,128)}) %all-gather.9.cloned.1.call-update) | async-done | bytes 4194320 | tf_op jit(solution)/shard_map/all_gather | solution.py:21
  95.4 2.7 reduce_sum.72
  98.2 21.4 %all-gather.7.cloned.1.call-done = bf16[512,1024]{1,0:T(8,128)(2,1)} async-done(((bf16[64,1024]{1,0:T(8,128)(2,1)}), bf16[512,1024]{1,0:T(8,128)(2,1)}) %all-gather.7.cloned.1.call-update) | async-done | bytes 1048592 | tf_op jit(solution)/shard_map/all_gather | solution.py:30
  119.7 2.6 fusion.17
  122.3 15.4 %all-reduce = (f32[512]{0:T(512)S(1)}, f32[512]{0:T(512)S(1)}) all-reduce(f32[512]{0:T(512)S(1)} %get-tuple-element.8, f32[512]{0:T(512)S(1)} %get-tuple-element.10), channel_id=1, replica_groups=mesh['dp'=4,'row'=2,'col'=4] {'dp','row'}, use_global_device_ids=true, to_apply=%region_10.11 | all-reduce | flops 1024 | bytes 8192 | tf_op jit(solution)/shard_map/psum | solution.py:42
  137.6 9.7 %all-reduce.1 = (f32[256]{0:T(256)S(1)}, f32[256]{0:T(256)S(1)}) all-reduce(f32[256]{0:T(256)S(1)} %get-tuple-element.9, f32[256]{0:T(256)S(1)} %get-tuple-element.11), channel_id=1, replica_groups=mesh['dp'=4,'row'=2,'col'=4] {'col'}, use_global_device_ids=true, to_apply=%region_6.7 | all-reduce | flops 512 | bytes 4096 | tf_op jit(solution)/shard_map/psum | solution.py:41
  147.3 2.9 convolution_multiply_fusion
  150.3 49.0 %all-reduce.4.cloned.1.call-done = f32[256,1024]{1,0:T(8,128)} async-done(((f32[256,1024]{1,0:T(8,128)}), f32[256,1024]{1,0:T(8,128)}) %all-reduce.4.cloned.1.call-update) | async-done | bytes 1048592 | tf_op jit(solution)/shard_map/psum | solution.py:49
  199.3 1.6 multiply_reduce_fusion
  200.9 1.0 multiply_convert_fusion
  201.9 11.2 %convolution_bitcast_fusion = f32[4096,1024]{0,1:T(8,128)} fusion(bf16[256,4096]{1,0:T(8,128)(2,1)} %param.5, f32[256,1024]{1,0:T(8,128)} %copy-done.3, bf16[256,1024]{1,0:T(8,128)(2,1)} %multiply_convert_fusion, bf16[1024,1024]{1,0:T(8,128)(2,1)S(1)} %copy-done), kind=kOutput, calls=%fused_computation | convolution fusion | flops 2689597440 | bytes 22544384 | tf_op jit(solution)/shard_map/dot_general | solution.py:61
  213.2 1.0 copy-done.1
  214.2 4.0 fusion.47
  218.3 0.6 dynamic_slice.3
  218.9 0.6 log_subtract_fusion.1
  219.4 162.1 %reduce-scatter.3.cloned.1.call-done = f32[512,1024]{0,1:T(8,128)} async-done(((f32[4096,1024]{0,1:T(8,128)}), f32[512,1024]{0,1:T(8,128)}) %reduce-scatter.3.cloned.1.call-update) | async-done | bytes 2097168 | tf_op jit(solution)/shard_map/reduce_scatter | solution.py:60
  381.6 2.9 copy.9
  384.4 48.2 %reduce-scatter.5.cloned.1.call-done = f32[1024,128]{1,0:T(8,128)} async-done(((f32[1024,1024]{1,0:T(8,128)}), f32[1024,128]{1,0:T(8,128)}) %reduce-scatter.5.cloned.1.call-update) | async-done | bytes 524304 | tf_op jit(solution)/shard_map/reduce_scatter | solution.py:58
  (27 shorter events, 0.7 us)
Async XLA Ops:
  7.2 32.3 %copy-start = (bf16[1024,1024]{1,0:T(8,128)(2,1)S(1)}, bf16[1024,1024]{1,0:T(8,128)(2,1)}, u32[]{:S(2)}) copy-start(bf16[1024,1024]{1,0:T(8,128)(2,1)} %param.7) | copy-start | bytes 6291460
  7.2 25.0 %all-gather.5.cloned.1.call-start = ((), (), s32[]{:S(2)}) async-start(), calls=%async_computation.2 | async-start | bytes 12582912 | tf_op jit(solution)/shard_map/all_gather | solution.py:17
  7.9 87.4 %all-gather.9.cloned.1.call-start = ((), (), s32[]{:S(2)}) async-start(), calls=%async_computation.7 | async-start | bytes 5242880 | tf_op jit(solution)/shard_map/all_gather | solution.py:21
  38.5 1.0 copy-start.3
  39.5 1.9 copy-start.4
  41.3 78.3 %all-gather.7.cloned.1.call-start = ((), (), s32[]{:S(2)}) async-start(), calls=%async_computation.3 | async-start | bytes 1179648 | tf_op jit(solution)/shard_map/all_gather | solution.py:30
  42.3 157.0 %all-reduce.4.cloned.1.call-start = ((), (), s32[]{:S(2)}) async-start(), calls=%async_computation.4 | async-start | bytes 2097152 | tf_op jit(solution)/shard_map/psum | solution.py:49
  95.4 24.3 %copy-start.5 = (s32[256]{0:T(256)S(1)}, s32[256]{0:T(256)}, u32[]{:S(2)}) copy-start(s32[256]{0:T(256)} %param.9) | copy-start | bytes 3076
  150.3 231.3 %reduce-scatter.3.cloned.1.call-start = ((), (), s32[]{:S(2)}) async-start(), calls=%async_computation.5 | async-start | bytes 18874368 | tf_op jit(solution)/shard_map/reduce_scatter | solution.py:60
  199.3 1.6 copy-start.2
  213.1 1.0 copy-start.1
  213.2 219.5 %reduce-scatter.5.cloned.1.call-start = ((), (), s32[]{:S(2)}) async-start(), calls=%async_computation.6 | async-start | bytes 4718592 | tf_op jit(solution)/shard_map/reduce_scatter | solution.py:58
Sparse Core Ops, SparseCore 0:
  9.6 22.5 all-gather.4
  41.5 53.8 all-gather.8
  97.5 22.0 all-gather.6
  150.4 48.8 all-reduce.3
  213.3 168.2 reduce-scatter.2
  384.3 48.3 reduce-scatter.4
